TPU v7x, 512 devices: a whole 4x4x16 slice. The times are simulated.
512 devices in a mesh: ctx: 64 (over z_lo, x, core), dp: 8 (over z_hi, y).
Axes of the slice: x: 4, y: 4, z: 16 (z_hi: 2, z_lo: 8; z = z_hi * 8 + z_lo), core: 2. Of those that a mesh axis runs over, the one named last changes fastest.
Arguments:
- queries: bfloat16 [8, 8192, 2048], P('dp', 'ctx'), may hold values from -28 to 28
- keys: bfloat16 [8, 8192, 2048], P('dp', 'ctx'), may hold values from -28 to 28
- values: bfloat16 [8, 8192, 2048], P('dp', 'ctx'), may hold values from -6 to 6
- saved_output: bfloat16 [8, 8192, 2048], P('dp', 'ctx'), may hold values from -6 to 6
- d_out: bfloat16 [8, 8192, 2048], P('dp', 'ctx'), may hold values from -16 to 16
- w_out: bfloat16 [2048, 2048], P('dp', 'ctx'), may hold values from -0.125 to 0.125
- block_order: int32 [128], replicated, may hold values from 0 to 127, each once
Outputs:
- d_queries: bfloat16 [8, 8192, 2048], P('dp', 'ctx')
- d_keys: bfloat16 [8, 8192, 2048], P('dp', 'ctx')
- d_values: bfloat16 [8, 8192, 2048], P('dp', 'ctx')
- d_wo: float32 [2048, 2048], P('dp', 'ctx')
All inputs are finite; a program needn't handle non-finite values.
Results may differ from a plain program's by a relative error of at most 0.0057.
Values may be sent and summed in bfloat16 or wider, within the bound.
A program may use at most 64 MiB of HBM per device.

v0:
```python
import math

import jax
import jax.numpy as jnp
from jax import lax
from jax.sharding import PartitionSpec as P

DH = 128
HOPS = 2


def passed_along(x, axis, by):
    length = lax.axis_size(axis)
    return lax.ppermute(x, axis, [(i, (i + by) % length) for i in range(length)])


def block_places(block_order, group, tok):
    pair = lax.dynamic_slice_in_dim(block_order, 2 * group, 2)
    row_ids = jnp.arange(tok, dtype=jnp.int32)
    half_block = tok // 2
    first = jnp.where(row_ids < half_block, pair[0], pair[1])
    return first * half_block + row_ids % half_block


def masked_scores(query_heads, key_heads, allowed, score_scale):
    scores = (
        jnp.einsum("qhd,khd->hqk", query_heads, key_heads, preferred_element_type=jnp.float32)
        * score_scale
    )
    return jnp.where(allowed[None, :, :], scores, -1e30)


def block_grads(query_heads, grad_heads, key_heads, value_heads, masked, lse, delta, score_scale):
    probs = jnp.exp(masked - lse[..., None])
    probs_low = probs.astype(jnp.bfloat16)
    d_probs = jnp.einsum(
        "qhd,khd->hqk", grad_heads, value_heads, preferred_element_type=jnp.float32
    )
    d_scores = (probs * (d_probs - delta[..., None])).astype(jnp.bfloat16)
    d_query = (
        jnp.einsum("hqk,khd->qhd", d_scores, key_heads, preferred_element_type=jnp.float32)
        * score_scale
    )
    d_key = (
        jnp.einsum("hqk,qhd->khd", d_scores, query_heads, preferred_element_type=jnp.float32)
        * score_scale
    )
    d_value = jnp.einsum("hqk,qhd->khd", probs_low, grad_heads, preferred_element_type=jnp.float32)
    return (d_query, d_key, d_value)


def per_device(queries, keys, values, saved_output, d_out, w_out, block_order):
    ctx_count = lax.axis_size("ctx")
    dp_count = lax.axis_size("dp")
    group = lax.axis_index("ctx")
    tok = queries.shape[1]
    head_feat = queries.shape[2]
    heads = head_feat // DH
    slice_width = head_feat // dp_count
    score_scale = 1.0 / math.sqrt(DH)
    all_grads = lax.all_gather(d_out, "dp", axis=0, tiled=True)
    all_saved = lax.all_to_all(saved_output, "dp", split_axis=2, concat_axis=0, tiled=True)
    grads_flat = all_grads.reshape(-1, all_grads.shape[2])
    saved_flat = all_saved.reshape(-1, slice_width)
    row_weight = lax.all_gather(w_out, "ctx", axis=1, tiled=True)
    partial_attn = lax.dot_general(
        grads_flat, row_weight, (((1,), (1,)), ((), ())), preferred_element_type=jnp.float32
    )
    lowered = partial_attn.astype(jnp.bfloat16).reshape(dp_count, tok, slice_width)
    d_attn = lax.all_to_all(lowered, "dp", split_axis=0, concat_axis=2, tiled=True)[0]
    wo_term = lax.dot_general(
        grads_flat, saved_flat, (((0,), (0,)), ((), ())), preferred_element_type=jnp.float32
    )
    wo_part = lax.psum_scatter(wo_term, "ctx", scatter_dimension=0, tiled=True)
    grad_scale = 1.0 / math.sqrt(dp_count * ctx_count * tok)
    d_wo = wo_part.T * grad_scale
    query_places = block_places(block_order, group, tok)
    query_heads = queries[0].reshape(tok, heads, DH)
    grad_heads = d_attn.reshape(tok, heads, DH)
    saved_heads = saved_output[0].reshape(tok, heads, DH)
    delta = jnp.sum(grad_heads.astype(jnp.float32) * saved_heads.astype(jnp.float32), axis=-1).T
    own_pair = (keys[0], values[0])
    collected = [own_pair]
    travelling = own_pair
    for distance in range(HOPS):
        travelling = passed_along((travelling[0], travelling[1]), "ctx", 1)
        collected.append(travelling)
    key_all = jnp.concatenate([entry[0] for entry in collected], axis=0).reshape(-1, heads, DH)
    value_all = jnp.concatenate([entry[1] for entry in collected], axis=0).reshape(-1, heads, DH)
    key_places = jnp.concatenate(
        [
            block_places(block_order, (group - distance) % ctx_count, tok)
            for distance in range(HOPS + 1)
        ],
        axis=0,
    )
    allowed = key_places[None, :] <= query_places[:, None]
    masked = masked_scores(query_heads, key_all, allowed, score_scale)
    row_max = jnp.max(masked, axis=-1)
    lse = row_max + jnp.log(jnp.sum(jnp.exp(masked - row_max[..., None]), axis=-1))
    d_query, d_key_all, d_value_all = block_grads(
        query_heads, grad_heads, key_all, value_all, masked, lse, delta, score_scale
    )
    d_key_all = d_key_all.reshape(-1, head_feat)
    d_value_all = d_value_all.reshape(-1, head_feat)
    grad_parts = [
        (
            d_key_all[distance * tok : (distance + 1) * tok],
            d_value_all[distance * tok : (distance + 1) * tok],
        )
        for distance in range(HOPS + 1)
    ]
    running = grad_parts[HOPS]
    for distance in range(HOPS, 0, -1):
        running = passed_along(running, "ctx", -1)
        if distance > 1:
            running = (
                running[0] + grad_parts[distance - 1][0],
                running[1] + grad_parts[distance - 1][1],
            )
    d_key = (grad_parts[0][0] + running[0]).astype(jnp.bfloat16)
    d_value = (grad_parts[0][1] + running[1]).astype(jnp.bfloat16)
    d_query = d_query.reshape(tok, head_feat)
    d_query = d_query.astype(jnp.bfloat16)
    return (d_query[None], d_key[None], d_value[None], d_wo)


def solution(mesh):
    in_specs = (
        P("dp", "ctx", None),
        P("dp", "ctx", None),
        P("dp", "ctx", None),
        P("dp", "ctx", None),
        P("dp", "ctx", None),
        P("dp", "ctx"),
        P(),
    )
    out_specs = (P("dp", "ctx", None), P("dp", "ctx", None), P("dp", "ctx", None), P("dp", "ctx"))
    return jax.shard_map(
        per_device, mesh=mesh, in_specs=in_specs, out_specs=out_specs, check_vma=False
    )
```

profile of v0, /device:TPU:1, one launch (start us, length us, event | category | flops | bytes accessed | tf_op | source)
XLA Modules:
  0.0 807.6 jit_solution(6477085316538706059)
XLA Ops:
  8.7 2.4 copy.111
  11.6 11.5 %reduce = bf16[2048,128]{1,0:T(8,128)(2,1)S(1)} reduce(bf16[2048,1,128]{2,1,0:T(2,128)(2,1)S(1)} %bitcast.77, bf16[]{:T(256)} %broadcast.92), dimensions={1}, to_apply=%bitcast.64.reduce_sub_computation | reduce | bytes 1048578
  24.1 18.3 %all-to-all-start.1 = ((bf16[8,2,16384]{2,1,0:T(2,128)(2,1)}), bf16[8,2,16384]{2,1,0:T(2,128)(2,1)S(1)}, u32[]{:S(2)}, u32[]{:S(2)}) async-start(bf16[8,2,16384]{2,1,0:T(2,128)(2,1)} %reshape.109), calls=%async_computation.1 | async-start | bytes 1048576 | tf_op jit(solution)/shard_map/all_to_all | solution.py:62
  42.6 4.0 collective-permute-start.2
  58.0 3.5 collective-permute-start.3
  63.4 95.1 %all-gather.5.cloned.1.call-done = bf16[256,2048]{0,1:T(8,128)(2,1)} async-done(((bf16[256,32]{0,1:T(8,128)(2,1)}), bf16[256,2048]{0,1:T(8,128)(2,1)}) %all-gather.5.cloned.1.call-update) | async-done | bytes 1048592 | tf_op jit(solution)/shard_map/all_gather | solution.py:65
  158.5 177.5 %all-gather.3.cloned.1.call-done = bf16[8,128,2048]{2,1,0:T(8,128)(2,1)} async-done(((bf16[1,128,2048]{2,1,0:T(8,128)(2,1)}), bf16[8,128,2048]{2,1,0:T(8,128)(2,1)}) %all-gather.3.cloned.1.call-update) | async-done | bytes 4194320 | tf_op jit(solution)/shard_map/all_gather | solution.py:61
  336.0 3.7 convolution_convert_fusion
  340.8 4.2 all-to-all-start
  353.0 2.1 fusion.1
  355.9 3.5 reshape.110
  363.5 5.0 fusion.29
  370.9 2.6 multiply_convert_fusion
  375.9 2.5 copy.105
  378.5 6.0 collective-permute-start.4
  391.4 4.3 collective-permute-done.4
  395.7 2.3 bitcast_add_fusion
  398.0 3.4 collective-permute-start.5
  401.8 5.5 collective-permute-done.6
  407.3 2.4 add.98
  409.7 7.4 collective-permute-start.7
  423.7 6.2 collective-permute-done.7
  429.8 2.1 fusion.16
  432.0 367.7 %reduce-scatter.2.cloned.1.call-done = f32[32,256]{1,0:T(8,128)} async-done(((f32[2048,256]{1,0:T(8,128)}), f32[32,256]{1,0:T(8,128)}) %reduce-scatter.2.cloned.1.call-update) | async-done | bytes 32784 | tf_op jit(solution)/shard_map/reduce_scatter | solution.py:74
  (85 shorter events, 50.3 us)
Async XLA Ops:
  7.2 35.2 %copy-start.8 = (bf16[1,128,2048]{2,1,0:T(8,128)(2,1)S(1)}, bf16[1,128,2048]{2,1,0:T(8,128)(2,1)}, u32[]{:S(2)}) copy-start(bf16[1,128,2048]{2,1,0:T(8,128)(2,1)} %param.9) | copy-start | bytes 1572868
  7.2 151.3 %all-gather.5.cloned.1.call-start = ((), (), s32[]{:S(2)}) async-start(), calls=%async_computation.4 | async-start | bytes 1064960 | tf_op jit(solution)/shard_map/all_gather | solution.py:65
  7.9 328.1 %all-gather.3.cloned.1.call-start = ((), (), s32[]{:S(2)}) async-start(), calls=%async_computation.3 | async-start | bytes 4718592 | tf_op jit(solution)/shard_map/all_gather | solution.py:61
  8.7 37.9 %copy-start.9 = (bf16[1,128,2048]{2,1,0:T(8,128)(2,1)S(1)}, bf16[1,128,2048]{2,1,0:T(8,128)(2,1)}, u32[]{:S(2)}) copy-start(bf16[1,128,2048]{2,1,0:T(8,128)(2,1)} %param.8) | copy-start | bytes 1572868
  11.1 37.8 %copy-start.3 = (bf16[1,128,2048]{2,1,0:T(8,128)(2,1)S(1)}, bf16[1,128,2048]{2,1,0:T(8,128)(2,1)}, u32[]{:S(2)}) copy-start(bf16[1,128,2048]{2,1,0:T(8,128)(2,1)} %param.10) | copy-start | bytes 1572868
  24.1 316.7 %all-to-all-start.1 = ((bf16[8,2,16384]{2,1,0:T(2,128)(2,1)}), bf16[8,2,16384]{2,1,0:T(2,128)(2,1)S(1)}, u32[]{:S(2)}, u32[]{:S(2)}) async-start(bf16[8,2,16384]{2,1,0:T(2,128)(2,1)} %reshape.109), calls=%async_computation.1 | async-start | bytes 1048576 | tf_op jit(solution)/shard_map/all_to_all | solution.py:62
  42.3 11.6 %copy-start.13 = (s32[128]{0:T(128)S(1)}, s32[128]{0:T(128)}, u32[]{:S(2)}) copy-start(s32[128]{0:T(128)} %param.13) | copy-start | bytes 1540
  42.6 15.4 %collective-permute-start.2 = (bf16[128,2048]{0,1:T(8,128)(2,1)S(1)}, bf16[128,2048]{0,1:T(8,128)(2,1)}, u32[]{:S(2)}, u32[]{:S(2)}) collective-permute-start(bf16[128,2048]{0,1:T(8,128)(2,1)S(1)} %bitcast.87), channel_id=1, source_target_pairs={{0,8},{8,16},{16,24},{24,32},{32,40},{40,48},{48,56},{56,64},{64,7... | collective-permute-start | bytes 1572872 | tf_op jit(solution)/shard_map/ppermute | solution.py:14
  46.9 14.6 %collective-permute-start = (bf16[128,2048]{0,1:T(8,128)(2,1)S(1)}, bf16[128,2048]{0,1:T(8,128)(2,1)S(1)}, u32[]{:S(2)}, u32[]{:S(2)}) collective-permute-start(bf16[128,2048]{0,1:T(8,128)(2,1)S(1)} %bitcast.85), channel_id=1, source_target_pairs={{0,8},{8,16},{16,24},{24,32},{32,40},{40,48},{48,56},{56,64},{64,7... | collective-permute-start | bytes 1572872 | tf_op jit(solution)/shard_map/ppermute | solution.py:14
  58.0 293.0 %collective-permute-start.3 = (bf16[128,2048]{0,1:T(8,128)(2,1)}, bf16[128,2048]{0,1:T(8,128)(2,1)S(1)}, u32[]{:S(2)}, u32[]{:S(2)}) collective-permute-start(bf16[128,2048]{0,1:T(8,128)(2,1)} %collective-permute-done.2), channel_id=1, source_target_pairs={{0,8},{8,16},{16,24},{24,32},{32,40},{40,48},{48,56},{56,64},{64,7... | collective-permute-start | bytes 1572872 | tf_op jit(solution)/shard_map/ppermute | solution.py:14
  61.5 290.5 %collective-permute-start.1 = (bf16[128,2048]{0,1:T(8,128)(2,1)S(1)}, bf16[128,2048]{0,1:T(8,128)(2,1)S(1)}, u32[]{:S(2)}, u32[]{:S(2)}) collective-permute-start(bf16[128,2048]{0,1:T(8,128)(2,1)S(1)} %collective-permute-done), channel_id=1, source_target_pairs={{0,8},{8,16},{16,24},{24,32},{32,40},{40,48},{48,56},{56,64},{64,7... | collective-permute-start | bytes 1572872 | tf_op jit(solution)/shard_map/ppermute | solution.py:14
  340.8 12.2 %copy-start.4 = (bf16[8,2,16384]{2,1,0:T(2,128)(2,1)}, bf16[8,2,16384]{2,1,0:T(2,128)(2,1)S(1)}, u32[]{:S(2)}) copy-start(bf16[8,2,16384]{2,1,0:T(2,128)(2,1)S(1)} %all-to-all-done.1) | copy-start | bytes 1572868
  340.8 28.7 %all-to-all-start = ((bf16[8,128,256]{1,2,0:T(8,128)(2,1)}), bf16[8,128,256]{1,2,0:T(8,128)(2,1)}, u32[]{:S(2)}, u32[]{:S(2)}) async-start(bf16[8,128,256]{1,2,0:T(8,128)(2,1)} %copy.90), calls=%async_computation | async-start | bytes 1048576 | tf_op jit(solution)/shard_map/all_to_all | solution.py:70
  345.0 454.7 %reduce-scatter.2.cloned.1.call-start = ((), (), s32[]{:S(2)}) async-start(), calls=%async_computation.5 | async-start | bytes 2129920 | tf_op jit(solution)/shard_map/reduce_scatter | solution.py:74
  378.5 17.2 %collective-permute-start.4 = (f32[128,2048]{0,1:T(8,128)}, f32[128,2048]{0,1:T(8,128)}, u32[]{:S(2)}, u32[]{:S(2)}) collective-permute-start(f32[128,2048]{0,1:T(8,128)} %bitcast.90), channel_id=1, source_target_pairs={{0,504},{8,0},{16,8},{24,16},{32,24},{40,32},{48,40},{56,48},{64,5... | collective-permute-start | bytes 3145736 | tf_op jit(solution)/shard_map/ppermute | solution.py:14
  389.2 18.1 %collective-permute-start.6 = (f32[128,2048]{1,0:T(8,128)}, f32[128,2048]{1,0:T(8,128)}, u32[]{:S(2)}, u32[]{:S(2)}) collective-permute-start(f32[128,2048]{1,0:T(8,128)} %copy.108), channel_id=1, source_target_pairs={{0,504},{8,0},{16,8},{24,16},{32,24},{40,32},{48,40},{56,48},{64,5... | collective-permute-start | bytes 3145736 | tf_op jit(solution)/shard_map/ppermute | solution.py:14
  391.4 10.0 %copy-start.2 = (f32[128,16,128]{0,2,1:T(8,128)S(1)}, f32[128,16,128]{0,2,1:T(8,128)}, u32[]{:S(2)}) copy-start(f32[128,16,128]{0,2,1:T(8,128)} %get-tuple-element.20) | copy-start | bytes 3145732
  398.0 23.3 %collective-permute-start.5 = (f32[128,2048]{0,1:T(8,128)}, f32[128,2048]{0,1:T(8,128)}, u32[]{:S(2)}, u32[]{:S(2)}) collective-permute-start(f32[128,2048]{0,1:T(8,128)} %bitcast_add_fusion), channel_id=1, source_target_pairs={{0,504},{8,0},{16,8},{24,16},{32,24},{40,32},{48,40},{56,48},{64,5... | collective-permute-start | bytes 3145736 | tf_op jit(solution)/shard_map/ppermute | solution.py:14
  401.8 15.3 %copy-start.7 = (bf16[16,128,384]{1,2,0:T(8,128)(2,1)S(1)}, bf16[16,128,384]{1,2,0:T(8,128)(2,1)}, u32[]{:S(2)}) copy-start(bf16[16,128,384]{1,2,0:T(8,128)(2,1)} %copy-done.6) | copy-start | bytes 4718596
  401.8 15.3 %copy-start.10 = (bf16[128,16,128]{2,0,1:T(8,128)(2,1)S(1)}, bf16[128,16,128]{2,0,1:T(8,128)(2,1)}, u32[]{:S(2)}) copy-start(bf16[128,16,128]{2,0,1:T(8,128)(2,1)} %copy.86) | copy-start | bytes 1572868
  401.8 15.3 %copy-start.11 = (bf16[128,16,128]{2,0,1:T(8,128)(2,1)S(1)}, bf16[128,16,128]{2,0,1:T(8,128)(2,1)}, u32[]{:S(2)}) copy-start(bf16[128,16,128]{2,0,1:T(8,128)(2,1)} %copy.87) | copy-start | bytes 1572868
  401.8 15.3 %copy-start.12 = (bf16[128,16,128]{2,0,1:T(8,128)(2,1)S(1)}, bf16[128,16,128]{2,0,1:T(8,128)(2,1)}, u32[]{:S(2)}) copy-start(bf16[128,16,128]{2,0,1:T(8,128)(2,1)} %copy.88) | copy-start | bytes 1572868
  409.7 11.3 %copy-start = (f32[128,16,128]{2,0,1:T(8,128)S(1)}, f32[128,16,128]{2,0,1:T(8,128)}, u32[]{:S(2)}) copy-start(f32[128,16,128]{2,0,1:T(8,128)} %get-tuple-element.23) | copy-start | bytes 3145732
  409.7 20.1 %collective-permute-start.7 = (f32[128,2048]{1,0:T(8,128)}, f32[128,2048]{1,0:T(8,128)}, u32[]{:S(2)}, u32[]{:S(2)}) collective-permute-start(f32[128,2048]{1,0:T(8,128)} %add.98), channel_id=1, source_target_pairs={{0,504},{8,0},{16,8},{24,16},{32,24},{40,32},{48,40},{56,48},{64,5... | collective-permute-start | bytes 3145736 | tf_op jit(solution)/shard_map/ppermute | solution.py:14
  (3 other events, 9.7 us)
Sparse Core Ops, SparseCore 0:
  10.2 148.2 all-gather.4
  161.7 174.2 all-gather.2
  368.6 431.0 reduce-scatter.1
where the time goes:
time: 818 us; the launch traced here: 808 us
  waiting for transfers between devices  659 us (81%)
  starting transfers between devices  52.7 us (6%)
  local copies, waits for them, and re-layouts  36.2 us (4%)
  other arithmetic  28.4 us (3%)
  matrix products  17.4 us (2%)
  between operations  14.2 us (2%)
    reduce_scatter x1, waiting for transfers between devices, per_device(): wo_part = lax.psum_scatter(wo_term, 'ctx', scatter_dimension=0, tiled=True)  368 us
    all_gather x1, waiting for transfers between devices, per_device(): all_grads = lax.all_gather(d_out, 'dp', axis=0, tiled=True)  178 us
    all_gather x1, waiting for transfers between devices, per_device(): row_weight = lax.all_gather(w_out, 'ctx', axis=1, tiled=True)  95.1 us
    ppermute x8, starting transfers between devices, passed_along(): lax.ppermute(x, axis, [(i, (i + by) % length) for i in range(length)])  29.9 us
    all_to_all x1, starting transfers between devices, per_device(): lax.all_to_all(saved_output, 'dp', split_axis=2, concat_axis=0, tiled=True)  18.3 us
  transfers between devices with their start and end apart: 13, of which 7 were waited for; matrix products, arithmetic and copies ran while one was open for 10% of the time, Pallas kernels for 0%

commit v1 on v0

v1 whole, which is shorter than its diff:
```python
import math

import jax
import jax.numpy as jnp
from jax import lax
from jax.experimental import pallas as pl
from jax.experimental.pallas import tpu as pltpu
from jax.sharding import PartitionSpec as P

DH = 128
TOK = 128
HEADS = 16
FEAT = 2048
NX, NY, NZ, NZL = 4, 4, 16, 8
SLOTS = 2 * NY
MESH = pl.DeviceIdType.MESH
BF = jnp.bfloat16
F32 = jnp.float32

NT = (((1,), (1,)), ((), ()))
NN = (((1,), (0,)), ((), ()))
TN = (((0,), (0,)), ((), ()))


def dot(a, b, dims):
    return lax.dot_general(a, b, dims, preferred_element_type=F32)


def kernel(
    order_ref, q_in, k_in, v_in, saved_in, grad_in, wt_in,
    dq_ref, dk_ref, dv_ref, dw_ref,
    qb, kb, vb, sv, gb, dab, lse, delta,
    wt, sb, st, dsend, probs, probs_k, ds_own, bias,
    rs_out, rs_in, xs, xr,
    load_s, wx_s, wx_r, zw_s, zw_r, g_s, g_r, sa_s, sa_r, kv_s, kv_r, q_s, q_r,
    da_s, da_r, fw_s, fw_r, fo_s, fo_r, row_s, row_r, zr_s, zr_r, xr_s, xr_r,
):
    ctx = lax.axis_index("ctx")
    dp = lax.axis_index("dp")
    core = lax.rem(ctx, 2)
    x = lax.rem(lax.div(ctx, 2), NX)
    zl = lax.div(ctx, 2 * NX)
    y = lax.rem(dp, NY)
    z = lax.div(dp, NY) * NZL + zl
    n_ctx = 2 * NX * NZL
    me = 2 * y + core

    def at(xx, yy, zz, cc):
        return {
            "ctx": lax.rem(zz, NZL) * (2 * NX) + xx * 2 + cc,
            "dp": lax.div(zz, NZL) * NY + yy,
        }

    other = at(x, y, z, 1 - core)
    after = {"ctx": lax.rem(ctx + 2, n_ctx), "dp": dp}
    before = {"ctx": lax.rem(ctx + n_ctx - 2, n_ctx), "dp": dp}
    yp, ym, yf = lax.rem(y + 1, NY), lax.rem(y + 3, NY), lax.rem(y + 2, NY)
    y_up, y_down = at(x, yp, z, core), at(x, ym, z, core)
    z_up, z_down = at(x, y, lax.rem(z + 1, NZ), core), at(x, y, lax.rem(z + NZ - 1, NZ), core)
    y_group = [(dy, dc) for dy in (1, 3, 2, 0) for dc in (0, 1) if (dy, dc) != (0, 0)]
    x_group = [(dx, dc) for dx in (1, 3, 2, 0) for dc in (0, 1) if (dx, dc) != (0, 0)]

    def y_peer(dy, dc):
        yy, cc = lax.rem(y + dy, NY), lax.rem(core + dc, 2)
        return at(x, yy, z, cc), 2 * yy + cc

    def x_peer(dx, dc):
        xx, cc = lax.rem(x + dx, NX), lax.rem(core + dc, 2)
        return at(xx, y, z, cc), xx, cc

    def send(src, dst, ssem, rsem, device):
        copy = pltpu.make_async_remote_copy(
            src_ref=src, dst_ref=dst, send_sem=ssem, recv_sem=rsem, device_id=device, device_id_type=MESH
        )
        copy.start()

    def took(ref, sem):
        pltpu.make_async_copy(ref, ref, sem).wait()

    own = pl.ds(0, TOK)
    my_rows = pl.ds(pl.multiple_of(me * TOK, TOK), TOK)
    loads = [
        pltpu.make_async_copy(grad_in, gb.at[my_rows, :], load_s.at[0]),
        pltpu.make_async_copy(saved_in, sv, load_s.at[1]),
        pltpu.make_async_copy(k_in, kb.at[own, :], load_s.at[2]),
        pltpu.make_async_copy(q_in, qb.at[own, :], load_s.at[3]),
        pltpu.make_async_copy(v_in, vb.at[own, :], load_s.at[4]),
    ]
    for load in loads:
        load.start()

    barrier = pltpu.get_barrier_semaphore()
    peers = [y_peer(*d)[0] for d in y_group] + [x_peer(*d)[0] for d in x_group if d != (0, 1)]
    peers += [z_up, z_down, after, before]
    for peer in peers:
        pl.semaphore_signal(barrier, inc=1, device_id=peer, device_id_type=MESH)
    pl.semaphore_wait(barrier, len(peers))

    z_lanes = pl.ds(pl.multiple_of(lax.div(z, NZL) * DH, DH), DH)
    piece = pl.ds(pl.multiple_of(ctx * 32, 32), 32)
    for d in x_group:
        dev, xx, cc = x_peer(*d)
        send(wt_in.at[:, pl.ds(pl.multiple_of(cc * DH, DH), DH)], wt.at[piece, z_lanes], wx_s, wx_r, dev)
    wt[piece, z_lanes] = wt_in[:, pl.ds(pl.multiple_of(core * DH, DH), DH)]

    def half(slot, part):
        return gb.at[pl.ds(pl.multiple_of(slot * TOK + part * 64, 64), 64), :]

    def whole(slot):
        return gb.at[pl.ds(pl.multiple_of(slot * TOK, TOK), TOK), :]

    s_up, s_down, s_far = 2 * yp + core, 2 * ym + core, 2 * yf + core
    loads[0].wait()
    send(half(me, 0), half(me, 0), g_s.at[0], g_r.at[0], y_up)
    send(half(me, 1), half(me, 1), g_s.at[1], g_r.at[1], y_down)
    send(half(me, 1), half(me, 1), g_s.at[2], g_r.at[2], y_up)
    send(half(me, 0), half(me, 0), g_s.at[3], g_r.at[3], y_down)
    send(whole(me), whole(me), g_s.at[6], g_r.at[6], other)

    prev2, prev1 = pl.ds(2 * TOK, TOK), pl.ds(TOK, TOK)
    loads[2].wait()
    send(kb.at[own, :], kb.at[prev2, :], kv_s.at[0], kv_r.at[0], after)
    loads[3].wait()
    send(qb.at[own, :], qb.at[prev2, :], q_s.at[0], q_r.at[0], before)
    loads[4].wait()
    send(vb.at[own, :], vb.at[prev2, :], kv_s.at[1], kv_r.at[1], after)

    @pl.when(core == 0)
    def _():
        send(kb.at[own, :], kb.at[prev1, :], kv_s.at[2], kv_r.at[2], other)
        send(vb.at[own, :], vb.at[prev1, :], kv_s.at[3], kv_r.at[3], other)

    @pl.when(core == 1)
    def _():
        send(qb.at[own, :], qb.at[prev1, :], q_s.at[1], q_r.at[1], other)

    loads[1].wait()

    def head_lanes(h):
        return pl.ds(pl.multiple_of(h * DH, DH), DH)

    for d in y_group:
        dev, slot = y_peer(*d)
        for zh in range(2):
            send(sv.at[:, head_lanes(8 * zh + slot)], sb.at[my_rows, pl.ds(zh * DH, DH)], sa_s, sa_r, dev)
    for zh in range(2):
        sb[my_rows, pl.ds(zh * DH, DH)] = sv[:, head_lanes(8 * zh + me)]

    group = ctx
    lane = lax.broadcasted_iota(jnp.int32, (TOK, TOK), 1)
    row = lax.broadcasted_iota(jnp.int32, (TOK, TOK), 0)

    def places(g, index):
        first, second = order_ref[2 * g], order_ref[2 * g + 1]
        return jnp.where(index < 64, first * 64 + index, second * 64 + index - 64)

    def blocked(key_group, query_group):
        seen = places(key_group, row) <= places(query_group, lane)
        return jnp.where(seen, 0.0, -1e30).astype(F32)

    def shifted(by):
        return lax.rem(group + n_ctx + by, n_ctx)

    bias[0] = blocked(group, group)
    bias[1] = blocked(shifted(-1), group)
    bias[2] = blocked(shifted(-2), group)
    bias[3] = blocked(group, shifted(1))
    bias[4] = blocked(group, shifted(2))
    scale = 1.0 / math.sqrt(DH)

    def z_rows(zz, first=0, count=256):
        start = lax.rem(zz, NZL) * 256 + first
        return wt.at[
            pl.ds(pl.multiple_of(start, 128), count),
            pl.ds(pl.multiple_of(lax.div(zz, NZL) * DH, DH), DH),
        ]

    def ring_step(t):
        up = lax.rem(z + NZ - (t - 1), NZ)
        down = lax.rem(z + (t - 1), NZ)
        parts = (0, 256, 0, 256) if t < 8 else (0, 128, 128, 128)
        send(z_rows(up, *parts[:2]), z_rows(up, *parts[:2]), zw_s.at[0, t - 1], zw_r.at[0, t - 1], z_up)
        send(z_rows(down, *parts[2:]), z_rows(down, *parts[2:]), zw_s.at[1, t - 1], zw_r.at[1, t - 1], z_down)

    def ring_wait(sems, t):
        count = 256 if t < 8 else 128
        for way in range(2):
            took(wt.at[pl.ds(0, count), pl.ds(0, DH)], sems.at[way, t - 1])

    took(wt.at[pl.ds(0, 224), pl.ds(0, DH)], wx_r)
    for t in range(1, 9):
        ring_step(t)
        if t == 3:
            took(half(s_down, 0), g_r.at[0])
            send(half(s_down, 0), half(s_down, 0), g_s.at[4], g_r.at[4], y_up)
            took(half(s_up, 1), g_r.at[1])
            send(half(s_up, 1), half(s_up, 1), g_s.at[5], g_r.at[5], y_down)
        if t == 5:
            took(half(s_down, 1), g_r.at[2])
            send(whole(s_down), whole(s_down), g_s.at[7], g_r.at[7], other)
            took(half(s_up, 0), g_r.at[3])
            send(whole(s_up), whole(s_up), g_s.at[8], g_r.at[8], other)
        if t == 6:
            took(kb.at[prev2, :], kv_r.at[0])
            took(qb.at[prev2, :], q_r.at[0])

            @pl.when(core == 1)
            def _():
                send(kb.at[prev2, :], kb.at[prev1, :], kv_s.at[2], kv_r.at[2], other)

            @pl.when(core == 0)
            def _():
                send(qb.at[prev2, :], qb.at[prev1, :], q_s.at[1], q_r.at[1], other)
        ring_wait(zw_r, t)

    took(half(s_far, 0), g_r.at[4])
    took(half(s_far, 1), g_r.at[5])
    send(whole(s_far), whole(s_far), g_s.at[9], g_r.at[9], other)
    for i in range(6, 10):
        took(whole(me), g_r.at[i])

    for dy in (2, 1, 3, 0):
        yy = lax.rem(y + dy, NY)
        rows = pl.ds(pl.multiple_of(yy * 256, 256), 256)
        part = dot(gb[rows, :], wt[...], NN).astype(BF)
        for cc in range(2):
            slot = 2 * yy + cc
            for zh in range(2):
                dsend[slot, zh] = part[cc * TOK : (cc + 1) * TOK, zh * DH : (zh + 1) * DH]
            mine = dab.at[pl.ds(2 * me, 2), own, :]
            if dy != 0:
                send(dsend.at[slot], mine, da_s.at[2 * dy + cc], da_r.at[me], at(x, yy, z, cc))
        if dy == 0:
            send(dsend.at[2 * y + 1 - core], dab.at[pl.ds(2 * me, 2), own, :], da_s.at[0], da_r.at[me], other)
            for zh in range(2):
                dab[2 * me + zh, 0:TOK, :] = dsend[me, zh]

    took(kb.at[prev1, :], kv_r.at[2])

    def score_head(i, carry):
        h = 8 * lax.rem(i, 2) + lax.div(i, 2)
        lanes = head_lanes(h)
        s = dot(kb[:, lanes], qb[own, lanes], NT) * scale
        s = s + bias[0:3].reshape(3 * TOK, TOK)
        top = jnp.max(s, axis=0, keepdims=True)
        e = jnp.exp(s - top)
        total = jnp.sum(e, axis=0, keepdims=True)
        probs[i] = e * (1.0 / total)
        lse[0, i] = top + jnp.log(total)
        return carry

    lax.fori_loop(0, HEADS, score_head, 0)

    near, far = pl.ds(TOK, TOK), pl.ds(2 * TOK, TOK)
    send(lse.at[0], lse.at[2], row_s.at[0], row_r.at[0], before)

    @pl.when(core == 1)
    def _():
        send(lse.at[0], lse.at[1], row_s.at[1], row_r.at[1], other)

    took(vb.at[prev2, :], kv_r.at[1])

    @pl.when(core == 1)
    def _():
        send(vb.at[prev2, :], vb.at[prev1, :], kv_s.at[3], kv_r.at[3], other)

    took(sb.at[pl.ds(0, 896), :], sa_r)
    st[...] = sb[...].astype(F32).T.astype(BF)

    def partial_of(zz):
        zh, low = lax.div(zz, NZL), lax.rem(zz, NZL)
        return dot(
            st[pl.ds(pl.multiple_of(zh * DH, DH), DH), :],
            gb[:, pl.ds(pl.multiple_of(low * 256, 256), 256)],
            NN,
        )

    def sum_step(t):
        up = partial_of(lax.rem(z + 9 - t, NZ))
        if t > 1:
            took(rs_in.at[0, t - 2], zr_r.at[0, t - 2])
            up = up + rs_in[0, t - 2].astype(F32)
        rs_out[0, t - 1] = up.astype(BF)
        send(rs_out.at[0, t - 1], rs_in.at[0, t - 1], zr_s.at[0, t - 1], zr_r.at[0, t - 1], z_up)
        if t < 8:
            down = partial_of(lax.rem(z + NZ - 8 + t, NZ))
            if t > 1:
                took(rs_in.at[1, t - 2], zr_r.at[1, t - 2])
                down = down + rs_in[1, t - 2].astype(F32)
            rs_out[1, t - 1] = down.astype(BF)
            send(rs_out.at[1, t - 1], rs_in.at[1, t - 1], zr_s.at[1, t - 1], zr_r.at[1, t - 1], z_down)

    def chunk(slot, rows):
        return dab.at[pl.ds(2 * slot, 2), rows, :]

    def pass_on(dy, cc):
        slot = 2 * lax.rem(y + dy, NY) + cc
        if dy == 0:
            @pl.when(cc != core)
            def _():
                took(chunk(slot, own), da_r.at[slot])
        else:
            took(chunk(slot, own), da_r.at[slot])
        send(chunk(slot, own), chunk(slot, far), fw_s.at[slot], fw_r.at[slot], before)

        @pl.when(core == 1)
        def _():
            send(chunk(slot, own), chunk(slot, near), fo_s.at[slot], fo_r.at[slot], other)

    sum_step(1)
    for dy in (0, 1, 3):
        for cc in range(2):
            pass_on(dy, cc)
    sum_step(2)
    for cc in range(2):
        pass_on(2, cc)

    ones = jnp.ones((8, DH), BF)

    def delta_head(i, carry):
        h = 8 * lax.rem(i, 2) + lax.div(i, 2)
        prod = dab[i, 0:TOK, :].astype(F32) * sv[:, head_lanes(h)].astype(F32)
        high = prod.astype(BF)
        low = (prod - high.astype(F32)).astype(BF)
        sums = dot(ones, high, NT) + dot(ones, low, NT)
        delta[0, i] = sums[0:1]
        return carry

    lax.fori_loop(0, HEADS, delta_head, 0)
    send(delta.at[0], delta.at[2], row_s.at[2], row_r.at[2], before)

    @pl.when(core == 1)
    def _():
        send(delta.at[0], delta.at[1], row_s.at[3], row_r.at[3], other)

    sum_step(3)

    took(qb.at[near, :], q_r.at[1])
    took(lse.at[2], row_r.at[0])

    @pl.when(core == 0)
    def _():
        send(lse.at[2], lse.at[1], row_s.at[1], row_r.at[1], other)

    took(lse.at[1], row_r.at[1])

    def later_head(i, carry):
        h = 8 * lax.rem(i, 2) + lax.div(i, 2)
        lanes = head_lanes(h)
        s = dot(kb[own, lanes], qb[TOK:, lanes], NT) * scale
        s = s + jnp.concatenate([bias[3], bias[4]], axis=1)
        probs_k[i] = jnp.exp(s - jnp.concatenate([lse[1, i], lse[2, i]], axis=1))
        return carry

    lax.fori_loop(0, HEADS, later_head, 0)
    sum_step(4)

    took(vb.at[prev1, :], kv_r.at[3])

    def own_head(i, carry):
        h = 8 * lax.rem(i, 2) + lax.div(i, 2)
        lanes = head_lanes(h)
        dprobs = dot(vb[:, lanes], dab[i, 0:TOK, :], NT)
        ds = (probs[i] * (dprobs - delta[0, i])).astype(BF)
        ds_own[i] = ds[0:TOK]
        dq_ref[:, lanes] = (dot(ds, kb[:, lanes], TN) * scale).astype(BF)
        return carry

    lax.fori_loop(0, HEADS // 2, own_head, 0)
    sum_step(5)
    lax.fori_loop(HEADS // 2, HEADS, own_head, 0)
    sum_step(6)

    for dy in (0, 1, 3, 2):
        for cc in range(2):
            slot = 2 * lax.rem(y + dy, NY) + cc
            took(chunk(slot, far), fw_r.at[slot])

            @pl.when(core == 0)
            def _():
                send(chunk(slot, far), chunk(slot, near), fo_s.at[slot], fo_r.at[slot], other)
    took(delta.at[2], row_r.at[2])

    @pl.when(core == 0)
    def _():
        send(delta.at[2], delta.at[1], row_s.at[3], row_r.at[3], other)

    sum_step(7)
    for slot in range(SLOTS):
        took(chunk(slot, near), fo_r.at[slot])
    took(delta.at[1], row_r.at[3])
    sum_step(8)

    def key_head(i, carry):
        h = 8 * lax.rem(i, 2) + lax.div(i, 2)
        lanes = head_lanes(h)
        later = dab[i, TOK:, :]
        p = probs_k[i]
        dprobs = dot(vb[own, lanes], later, NT)
        ds = (p * (dprobs - jnp.concatenate([delta[1, i], delta[2, i]], axis=1))).astype(BF)
        dkey = dot(ds_own[i], qb[own, lanes], NN) + dot(ds, qb[TOK:, lanes], NN)
        dk_ref[:, lanes] = (dkey * scale).astype(BF)
        dval = dot(probs[i, 0:TOK, :].astype(BF), dab[i, 0:TOK, :], NN) + dot(p.astype(BF), later, NN)
        dv_ref[:, lanes] = dval.astype(BF)
        return carry

    lax.fori_loop(0, HEADS, key_head, 0)

    total = partial_of(z)
    took(rs_in.at[0, 7], zr_r.at[0, 7])
    total = total + rs_in[0, 7].astype(F32)
    took(rs_in.at[1, 6], zr_r.at[1, 6])
    total = total + rs_in[1, 6].astype(F32)
    xs[...] = total.T
    for d in x_group:
        dev, xx, cc = x_peer(*d)
        rows = pl.ds(pl.multiple_of((2 * xx + cc) * 32, 32), 32)
        send(xs.at[rows, :], xr.at[2 * x + core], xr_s, xr_r, dev)
    xr[2 * x + core] = xs[pl.ds(pl.multiple_of((2 * x + core) * 32, 32), 32), :]
    took(xr.at[pl.ds(0, 7)], xr_r)
    grad_scale = 1.0 / math.sqrt(8 * n_ctx * TOK)
    for cc in range(2):
        both = (xr[cc] + xr[2 + cc]) + (xr[4 + cc] + xr[6 + cc])
        dw_ref[cc * DH : (cc + 1) * DH, :] = (both * grad_scale).T

    took(wt.at[pl.ds(0, 224), pl.ds(0, DH)], wx_s)
    for t in range(1, 9):
        ring_wait(zw_s, t)
        took(rs_out.at[0, t - 1], zr_s.at[0, t - 1])
        if t < 8:
            took(rs_out.at[1, t - 1], zr_s.at[1, t - 1])
    for i in range(6):
        took(half(me, 0), g_s.at[i])
    for i in range(6, 10):
        took(whole(me), g_s.at[i])
    took(sb.at[pl.ds(0, 896), :], sa_s)
    for i in range(4):
        took(kb.at[own, :], kv_s.at[i])
        took(lse.at[0], row_s.at[i])
    for i in range(2):
        took(qb.at[own, :], q_s.at[i])
    for i in [0, 2, 3, 4, 5, 6, 7]:
        took(dsend.at[0], da_s.at[i])
    for slot in range(SLOTS):
        took(chunk(slot, own), fw_s.at[slot])
        took(chunk(slot, own), fo_s.at[slot])
    took(xr.at[pl.ds(0, 7)], xr_s)


def per_device(queries, keys, values, saved_output, d_out, w_out, block_order):
    sems = pltpu.SemaphoreType.DMA
    vmem = pltpu.VMEM
    tokens = jax.ShapeDtypeStruct((TOK, FEAT), BF)
    anywhere = pl.BlockSpec(memory_space=pl.ANY)
    inside = pl.BlockSpec(memory_space=pltpu.VMEM)
    dq, dk, dv, dw = pl.pallas_call(
        kernel,
        out_shape=(tokens, tokens, tokens, jax.ShapeDtypeStruct((256, 32), F32)),
        in_specs=[pl.BlockSpec(memory_space=pltpu.SMEM)] + [anywhere] * 5 + [inside],
        out_specs=(inside,) * 4,
        scratch_shapes=[
            vmem((3 * TOK, FEAT), BF),
            vmem((3 * TOK, FEAT), BF),
            vmem((3 * TOK, FEAT), BF),
            vmem((TOK, FEAT), BF),
            vmem((SLOTS * TOK, FEAT), BF),
            vmem((HEADS, 3 * TOK, DH), BF),
            vmem((3, HEADS, 1, TOK), F32),
            vmem((3, HEADS, 1, TOK), F32),
            vmem((FEAT, 2 * DH), BF),
            vmem((SLOTS * TOK, 2 * DH), BF),
            vmem((2 * DH, SLOTS * TOK), BF),
            vmem((SLOTS, 2, TOK, DH), BF),
            vmem((HEADS, 3 * TOK, TOK), F32),
            vmem((HEADS, TOK, 2 * TOK), F32),
            vmem((HEADS, TOK, TOK), BF),
            vmem((5, TOK, TOK), F32),
            vmem((2, 8, DH, 256), BF),
            vmem((2, 8, DH, 256), BF),
            vmem((256, DH), F32),
            vmem((8, 32, DH), F32),
            sems((5,)),
            sems,
            sems,
            sems((2, 8)),
            sems((2, 8)),
            sems((10,)),
            sems((10,)),
            sems,
            sems,
            sems((4,)),
            sems((4,)),
            sems((2,)),
            sems((2,)),
            sems((8,)),
            sems((8,)),
            sems((8,)),
            sems((8,)),
            sems((8,)),
            sems((8,)),
            sems((4,)),
            sems((4,)),
            sems((2, 8)),
            sems((2, 8)),
            sems,
            sems,
        ],
        compiler_params=pltpu.CompilerParams(
            collective_id=0, has_side_effects=True, vmem_limit_bytes=48 * 1024 * 1024
        ),
    )(block_order, queries[0], keys[0], values[0], saved_output[0], d_out[0], w_out.T)
    return dq[None], dk[None], dv[None], dw


def solution(mesh):
    tokens = P("dp", "ctx", None)
    return jax.shard_map(
        per_device,
        mesh=mesh,
        in_specs=(tokens,) * 5 + (P("dp", "ctx"), P()),
        out_specs=(tokens,) * 3 + (P("dp", "ctx"),),
        check_vma=False,
    )
```

time: 818 us -> 135 us (0.17); the launches traced: 808 us -> 134 us
  waiting for transfers between devices: 659 us -> 0 us
  Pallas kernels: 0 us -> 124 us
  starting transfers between devices: 52.7 us -> 0 us
  other arithmetic: 28.4 us -> 0 us
  local copies, waits for them, and re-layouts: 36.2 us -> 9.64 us
  matrix products: 17.4 us -> 0 us
  between operations: 14.2 us -> 0.66 us
    reduce_scatter x1 -> x0, waiting for transfers between devices: 368 us -> none  [per_device(): wo_part = lax.psum_scatter(wo_term, 'ctx', scatter_dimension=0, tiled=True)]
    all_gather x2 -> x0, waiting for transfers between devices: 273 us -> none  [the longest x1 178 us: per_device(): all_grads = lax.all_gather(d_out, 'dp', axis=0, tiled=True)]
    pallas_call x0 -> x1, Pallas kernels: none -> 124 us  [per_device(): pl.pallas_call(kernel, out_shape=(tokens, tokens, tokens, jax.ShapeDtypeS...]
    ppermute x8 -> x0, starting transfers between devices: 29.9 us -> none  [passed_along(): lax.ppermute(x, axis, [(i, (i + by) % length) for i in range(length)])]
    all_to_all x2 -> x0, starting transfers between devices: 22.4 us -> none  [the longest x1 18.3 us: per_device(): lax.all_to_all(saved_output, 'dp', split_axis=2, concat_axis=0, tiled=True)]
    dot_general x7 -> x0, matrix products: 17.4 us -> none  [the longest x1 4.97 us: per_device(): lax.dot_general(grads_flat, saved_flat, (((0,), (0,)), ((), ())), preferr...]
    ppermute x8 -> x0, waiting for transfers between devices: 15.9 us -> none  [passed_along(): lax.ppermute(x, axis, [(i, (i + by) % length) for i in range(length)])]
    unnamed x1 -> x0, other arithmetic: 11.5 us -> none
  transfers between devices with their start and end apart: 13 -> 0, of which waited for: 7 -> 0; matrix products, arithmetic and copies ran while one was open for 10% -> 0% of each run, Pallas kernels for 0% -> 0%
where the time goes in v1:
time: 135 us; the launch traced here: 134 us
  Pallas kernels  124 us (92%)
  local copies, waits for them, and re-layouts  9.64 us (7%)
    pallas_call x1, Pallas kernels, per_device(): pl.pallas_call(kernel, out_shape=(tokens, tokens, tokens, jax.ShapeDtypeS...  124 us
    unnamed x18, local copies, waits for them, and re-layouts  9.64 us

profile of v1, /device:TPU:1, one launch (start us, length us, event | category | flops | bytes accessed | tf_op | source)
XLA Modules:
  0.0 134.2 jit_solution(3752884513447734921)
XLA Ops:
  0.6 0.0 copy-start.6
  0.6 0.6 copy-done.6
  1.3 0.0 copy-start
  1.3 1.0 copy-done
  2.3 0.0 copy-start.1
  2.3 1.0 copy-done.1
  3.4 0.0 copy-start.2
  3.4 1.0 copy-done.2
  4.4 0.0 copy-start.3
  4.4 1.0 copy-done.3
  5.5 0.0 copy-start.4
  5.5 1.0 copy-done.4
  6.5 0.0 copy-start.5
  6.5 0.7 copy-done.5
  7.2 123.9 %shard_map.102 = (bf16[128,2048]{1,0:T(8,128)(2,1)S(1)}, bf16[128,2048]{1,0:T(8,128)(2,1)S(1)}, bf16[128,2048]{1,0:T(8,128)(2,1)S(1)}, f32[256,32]{1,0:T(8,128)S(1)}) custom-call(s32[128]{0:T(128)S(1)} %copy-done.6, bf16[128,2048]{1,0:T(8,128)(2,1)S(1)} %bitcast.12, bf16[128,2048]{1,0:T(8,128)(2,1)S(1)} %bitcast.13, bf16[128,2048]{1,0:T(8,128)(2,1)S(1)} %bitcast.14, ...), custom_call_target="tpu_custom_call" | custom-call | tf_op jit(solution)/shard_map/pallas_call | solution.py:456
  131.1 0.7 copy.11
  131.8 0.8 copy.15
  132.6 0.8 copy.16
  133.4 0.8 copy.17
Async XLA Ops:
  0.6 0.7 copy-start.6
  1.3 1.0 copy-start
  2.3 1.0 copy-start.1
  3.4 1.0 copy-start.2
  4.4 1.0 copy-start.3
  5.5 1.0 copy-start.4
  6.5 0.7 copy-start.5

commit v2 on v1

v2 whole, which is shorter than its diff:
```python
import math

import jax
import jax.numpy as jnp
from jax import lax
from jax.experimental import pallas as pl
from jax.experimental.pallas import tpu as pltpu
from jax.sharding import PartitionSpec as P

DH = 128
TOK = 128
HEADS = 16
FEAT = 2048
NX, NY, NZ, NZL = 4, 4, 16, 8
SLOTS = 2 * NY
Z_OFFSETS = (1, 15, 2, 14, 3, 13, 4, 12, 5, 11, 6, 10, 7, 9, 8)
MESH = pl.DeviceIdType.MESH
KQ, VV, KO, SA, UN = 1, 3, 2, 11, 4
BF = jnp.bfloat16
F32 = jnp.float32

NT = (((1,), (1,)), ((), ()))
NN = (((1,), (0,)), ((), ()))
TN = (((0,), (0,)), ((), ()))


def dot(a, b, dims):
    return lax.dot_general(a, b, dims, preferred_element_type=F32)


def kernel(
    order_ref, q_in, k_in, v_in, saved_in, grad_in, wt_in,
    dq_ref, dk_ref, dv_ref, dw_ref,
    qb, kb, vb, sv, gb, dab, lse, delta,
    wt, ww, sb, st, dsend, probs, probs_k, ds_own, bias,
    dwp, dwb, xin, xsum, zout, zin, near_sum, quarter_out, quarter_in, mine_f, fin, turned,
    load_s, wc_s, wc_r, wz_s, wz_r, wx_s, wx_r, g_s, g_r, sa_s, sa_r, kv_s, kv_r, q_s, q_r,
    da_s, da_r, fw_s, fw_r, fo_s, fo_r, row_s, row_r, ds_s, ds_r, dn_s, dn_r, rx_s, rx_r, rz_s, rz_r, rq_s, rq_r, rf_s, rf_r,
):
    ctx = lax.axis_index("ctx")
    dp = lax.axis_index("dp")
    core = lax.rem(ctx, 2)
    x = lax.rem(lax.div(ctx, 2), NX)
    zl = lax.div(ctx, 2 * NX)
    y = lax.rem(dp, NY)
    z = lax.div(dp, NY) * NZL + zl
    n_ctx = 2 * NX * NZL
    me = 2 * y + core
    zt, zq, zr = lax.div(z, NZL), lax.div(zl, 4), lax.rem(zl, 4)

    def at(xx, yy, zz, cc):
        return {
            "ctx": lax.rem(zz, NZL) * (2 * NX) + xx * 2 + cc,
            "dp": lax.div(zz, NZL) * NY + yy,
        }

    other = at(x, y, z, 1 - core)
    after = {"ctx": lax.rem(ctx + 2, n_ctx), "dp": dp}
    before = {"ctx": lax.rem(ctx + n_ctx - 2, n_ctx), "dp": dp}
    yp, ym, yf = lax.rem(y + 1, NY), lax.rem(y + 3, NY), lax.rem(y + 2, NY)
    y_up, y_down = at(x, yp, z, core), at(x, ym, z, core)
    y_group = [(dy, dc) for dy in (1, 3, 2, 0) for dc in (0, 1) if (dy, dc) != (0, 0)]
    x_group = [(dx, dc) for dx in (1, 3, 2, 0) for dc in (0, 1) if (dx, dc) != (0, 0)]

    def y_peer(dy, dc):
        yy, cc = lax.rem(y + dy, NY), lax.rem(core + dc, 2)
        return at(x, yy, z, cc), 2 * yy + cc

    def x_peer(dx, dc):
        xx, cc = lax.rem(x + dx, NX), lax.rem(core + dc, 2)
        return at(xx, y, z, cc), xx, cc

    def send(src, dst, ssem, rsem, device):
        copy = pltpu.make_async_remote_copy(
            src_ref=src, dst_ref=dst, send_sem=ssem, recv_sem=rsem, device_id=device, device_id_type=MESH
        )
        copy.start()

    def took(ref, sem):
        pltpu.make_async_copy(ref, ref, sem).wait()

    own = pl.ds(0, TOK)
    my_rows = pl.ds(pl.multiple_of(me * TOK, TOK), TOK)
    loads = [
        pltpu.make_async_copy(grad_in, gb.at[my_rows, :], load_s.at[0]),
        pltpu.make_async_copy(saved_in, sv, load_s.at[1]),
        pltpu.make_async_copy(k_in, kb.at[own, :], load_s.at[2]),
        pltpu.make_async_copy(q_in, qb.at[own, :], load_s.at[3]),
        pltpu.make_async_copy(v_in, vb.at[own, :], load_s.at[4]),
    ]
    for load in loads:
        load.start()

    barrier = pltpu.get_barrier_semaphore()
    peers = [y_peer(*d)[0] for d in y_group] + [x_peer(*d)[0] for d in x_group if d != (0, 1)]
    peers += [at(x, y, lax.rem(z + dz, NZ), core) for dz in Z_OFFSETS] + [after, before]
    for peer in peers:
        pl.semaphore_signal(barrier, inc=1, device_id=peer, device_id_type=MESH)
    pl.semaphore_wait(barrier, len(peers))

    def w_piece(xx, zz):
        return wt.at[lax.div(zz, NZL), lax.rem(zz, NZL), xx]

    def half_lanes(cc):
        return pl.ds(pl.multiple_of(cc * DH, DH), DH)

    zh = lax.div(z, NZL)
    piece = pl.ds(pl.multiple_of(core * 32, 32), 32)
    send(wt_in.at[:, half_lanes(1 - core)], wt.at[zh, zl, x, piece], wc_s, wc_r, other)
    wt[zh, zl, x, piece] = wt_in[:, half_lanes(core)]
    def half(slot, part):
        return gb.at[pl.ds(pl.multiple_of(slot * TOK + part * 64, 64), 64), :]

    def whole(slot):
        return gb.at[pl.ds(pl.multiple_of(slot * TOK, TOK), TOK), :]

    s_up, s_down, s_far = 2 * yp + core, 2 * ym + core, 2 * yf + core
    loads[0].wait()
    send(half(me, 0), half(me, 0), g_s.at[0], g_r.at[0], y_up)
    send(half(me, 1), half(me, 1), g_s.at[1], g_r.at[1], y_down)
    send(half(me, 1), half(me, 1), g_s.at[2], g_r.at[2], y_up)
    send(half(me, 0), half(me, 0), g_s.at[3], g_r.at[3], y_down)
    send(whole(me), whole(me), g_s.at[6], g_r.at[6], other)
    took(wt_in.at[:, pl.ds(0, DH)], wc_r)
    for dz in Z_OFFSETS:
        send(w_piece(x, z), w_piece(x, z), wz_s.at[dz], wz_r.at[dz], at(x, y, lax.rem(z + dz, NZ), core))

    prev2, prev1 = pl.ds(2 * TOK, TOK), pl.ds(TOK, TOK)
    loads[2].wait()
    loads[3].wait()
    loads[4].wait()
    loads[1].wait()

    def head_lanes(h):
        return pl.ds(pl.multiple_of(h * DH, DH), DH)

    for zh in range(2):
        sb[my_rows, pl.ds(zh * DH, DH)] = sv[:, head_lanes(8 * zh + me)]

    def at_place(n):
        if n == KQ:
            send(kb.at[own, :], kb.at[prev2, :], kv_s.at[0], kv_r.at[0], after)
            send(qb.at[own, :], qb.at[prev2, :], q_s.at[0], q_r.at[0], before)
        if n == VV:
            send(vb.at[own, :], vb.at[prev2, :], kv_s.at[1], kv_r.at[1], after)
        if n == KO:
            @pl.when(core == 0)
            def _():
                send(kb.at[own, :], kb.at[prev1, :], kv_s.at[2], kv_r.at[2], other)
                send(vb.at[own, :], vb.at[prev1, :], kv_s.at[3], kv_r.at[3], other)

            @pl.when(core == 1)
            def _():
                send(qb.at[own, :], qb.at[prev1, :], q_s.at[1], q_r.at[1], other)
        if n == SA:
            for d in y_group:
                dev, slot = y_peer(*d)
                for top in range(2):
                    send(sv.at[:, head_lanes(8 * top + slot)], sb.at[my_rows, pl.ds(top * DH, DH)], sa_s, sa_r, dev)

    at_place(0)

    group = ctx
    lane = lax.broadcasted_iota(jnp.int32, (TOK, TOK), 1)
    row = lax.broadcasted_iota(jnp.int32, (TOK, TOK), 0)

    def places(g, index):
        first, second = order_ref[2 * g], order_ref[2 * g + 1]
        return jnp.where(index < 64, first * 64 + index, second * 64 + index - 64)

    def blocked(key_group, query_group):
        seen = places(key_group, row) <= places(query_group, lane)
        return jnp.where(seen, 0.0, -1e30).astype(F32)

    def shifted(by):
        return lax.rem(group + n_ctx + by, n_ctx)

    bias[0] = blocked(group, group)
    bias[1] = blocked(shifted(-1), group)
    bias[2] = blocked(shifted(-2), group)
    bias[3] = blocked(group, shifted(1))
    bias[4] = blocked(group, shifted(2))
    scale = 1.0 / math.sqrt(DH)

    def own_scores(i, carry):
        lanes = head_lanes(8 * lax.rem(i, 2) + lax.div(i, 2))
        probs[i, 0:TOK] = dot(kb[own, lanes], qb[own, lanes], NT) * scale + bias[0]
        return carry

    lax.fori_loop(0, HEADS, own_scores, 0, unroll=UN)

    def z_peer(dz):
        return at(x, y, lax.rem(z + dz, NZ), core)

    def rest_of(d):
        return lax.rem(zr + d, 4)

    def w_across(zz):
        for i, dx in enumerate((1, 3, 2)):
            send(w_piece(x, zz), w_piece(x, zz), wx_s, wx_r, at(lax.rem(x + dx, NX), y, z, core))

    w_across(z)
    for i, dz in enumerate(Z_OFFSETS):
        zz = lax.rem(z + dz, NZ)
        took(w_piece(x, zz), wz_r.at[NZ - dz])
        w_across(zz)
        if KQ == 1 and i % 2 == 0:
            part = i // 2 * 16
            send(kb.at[pl.ds(part, 16), :], kb.at[pl.ds(2 * TOK + part, 16), :], kv_s.at[0], kv_r.at[0], after)
            send(qb.at[pl.ds(part, 16), :], qb.at[pl.ds(2 * TOK + part, 16), :], q_s.at[0], q_r.at[0], before)
        if i == 5:
            took(half(s_down, 0), g_r.at[0])
            send(half(s_down, 0), half(s_down, 0), g_s.at[4], g_r.at[4], y_up)
            took(half(s_up, 1), g_r.at[1])
            send(half(s_up, 1), half(s_up, 1), g_s.at[5], g_r.at[5], y_down)
            at_place(11)
    at_place(2)
    took(half(s_down, 1), g_r.at[2])
    send(whole(s_down), whole(s_down), g_s.at[7], g_r.at[7], other)
    took(half(s_up, 0), g_r.at[3])
    send(whole(s_up), whole(s_up), g_s.at[8], g_r.at[8], other)
    took(wt.at[:, :, pl.ds(0, 3)], wx_r)
    at_place(3)

    took(half(s_far, 0), g_r.at[4])
    took(half(s_far, 1), g_r.at[5])
    send(whole(s_far), whole(s_far), g_s.at[9], g_r.at[9], other)
    for i in range(6, 10):
        took(whole(me), g_r.at[i])

    ww[:, 0:DH] = wt[0].reshape(FEAT, DH)
    ww[:, DH:] = wt[1].reshape(FEAT, DH)
    def attn_step(j, carry):
        dy = 2 - j + 3 * lax.div(j, 2) - 2 * lax.div(j, 3)
        yy = lax.rem(y + dy, NY)
        rows = pl.ds(pl.multiple_of(yy * 256, 256), 256)
        part = dot(gb[rows, :], ww[...], NN).astype(BF)
        for cc in range(2):
            slot = 2 * yy + cc
            for top in range(2):
                dsend[slot, top] = part[cc * TOK : (cc + 1) * TOK, top * DH : (top + 1) * DH]

            @pl.when(slot != me)
            def _():
                send(
                    dsend.at[slot], dab.at[pl.ds(2 * me, 2), own, :], da_s.at[slot], da_r.at[me],
                    at(x, yy, z, cc),
                )
        return carry

    lax.fori_loop(0, 4, attn_step, 0)
    for top in range(2):
        dab[2 * me + top, 0:TOK, :] = dsend[me, top]

    at_place(4)
    took(sb.at[pl.ds(0, 896), :], sa_r)
    st[...] = sb[...].astype(F32).T.astype(BF)

    def part_lanes(part):
        return pl.ds(part * 1024, 1024)

    def partial_sums(low, carry):
        lanes = pl.ds(pl.multiple_of(low * 256, 256), 256)
        sums = dot(st[...], gb[:, lanes], NN).reshape(2, NX, 32, 256)
        dwp[:, :, :, lanes] = sums
        dwb[:, :, :, lanes] = sums.astype(BF)
        return carry

    for part in range(2):
        lax.fori_loop(4 * part, 4 * part + 4, partial_sums, 0)
        for dx in (1, 3, 2):
            xx = lax.rem(x + dx, NX)
            send(
                dwb.at[:, xx, :, part_lanes(part)], xin.at[part, dx], rx_s.at[part, dx], rx_r.at[part, dx],
                at(xx, y, z, core),
            )

    at_place(5)

    def over_z(part):
        sums = dwp[:, x, :, part_lanes(part)]
        for dx in (1, 3, 2):
            took(xin.at[part, dx], rx_r.at[part, dx])
            sums = sums + xin[part, dx].astype(F32)
        for top in range(2):
            for rest in range(4):
                block = sums[top, :, rest * 256 : (rest + 1) * 256]
                xsum[rest, part, top] = block
                zout[rest, part, top] = block.astype(BF)
        send(zout.at[rest_of(1), part], zin.at[0, part], rz_s.at[part, 0], rz_r.at[part, 0], z_peer(1))
        send(zout.at[rest_of(3), part], zin.at[1, part], rz_s.at[part, 1], rz_r.at[part, 1], z_peer(15))
        send(zout.at[rest_of(2), part, 0], zin.at[2, part, 0], rz_s.at[part, 2], rz_r.at[part, 2], z_peer(2))
        send(zout.at[rest_of(2), part, 1], zin.at[2, part, 1], rz_s.at[part, 3], rz_r.at[part, 3], z_peer(14))

    def over_quarters(part):
        for i in range(2):
            took(zin.at[i, part], rz_r.at[part, i])
            took(zin.at[2, part, i], rz_r.at[part, 2 + i])
        sums = xsum[zr, part]
        for i in range(3):
            sums = sums + zin[i, part].astype(F32)
        near_sum[part] = sums
        quarter_out[part] = sums.astype(BF)
        for top in range(2):
            @pl.when((zq != part) | (zt != top))
            def _():
                send(
                    quarter_out.at[part, top], quarter_in.at[zq, zt], rq_s.at[part, top], rq_r,
                    at(x, y, top * NZL + part * 4 + zr, core),
                )

    took(kb.at[prev2, :], kv_r.at[0])
    took(qb.at[prev2, :], q_r.at[0])

    @pl.when(core == 1)
    def _():
        send(kb.at[prev2, :], kb.at[prev1, :], kv_s.at[2], kv_r.at[2], other)

    @pl.when(core == 0)
    def _():
        send(qb.at[prev2, :], qb.at[prev1, :], q_s.at[1], q_r.at[1], other)

    took(kb.at[prev1, :], kv_r.at[2])

    def score_head(i, carry):
        h = 8 * lax.rem(i, 2) + lax.div(i, 2)
        lanes = head_lanes(h)
        s = dot(kb[TOK:, lanes], qb[own, lanes], NT) * scale + bias[1:3].reshape(2 * TOK, TOK)
        s = jnp.concatenate([probs[i, 0:TOK], s], axis=0)
        top = jnp.max(s, axis=0, keepdims=True)
        e = jnp.exp(s - top)
        total = jnp.sum(e, axis=0, keepdims=True)
        probs[i] = e * (1.0 / total)
        lse[0, i] = top + jnp.log(total)
        return carry

    lax.fori_loop(0, HEADS, score_head, 0, unroll=UN)

    near, far = pl.ds(TOK, TOK), pl.ds(2 * TOK, TOK)
    send(lse.at[0], lse.at[2], row_s.at[0], row_r.at[0], before)

    @pl.when(core == 1)
    def _():
        send(lse.at[0], lse.at[1], row_s.at[1], row_r.at[1], other)

    def chunk(slot, rows):
        return dab.at[pl.ds(2 * slot, 2), rows, :]

    ones = jnp.ones((8, DH), BF)

    def deltas(slot, which):
        return delta.at[which, pl.ds(2 * slot, 2)]

    def pass_on(slot):
        @pl.when(slot != me)
        def _():
            took(chunk(slot, own), da_r.at[slot])

        send(chunk(slot, own), chunk(slot, far), fw_s.at[slot], fw_r.at[slot], before)

        @pl.when(core == 1)
        def _():
            send(chunk(slot, own), chunk(slot, near), fo_s.at[slot], fo_r.at[slot], other)

        for zh in range(2):
            i = 2 * slot + zh
            prod = dab[i, 0:TOK, :].astype(F32) * sv[:, head_lanes(8 * zh + slot)].astype(F32)
            high = prod.astype(BF)
            low = (prod - high.astype(F32)).astype(BF)
            sums = dot(ones, high, NT) + dot(ones, low, NT)
            delta[0, i] = sums[0:1]
        send(deltas(slot, 0), deltas(slot, 2), ds_s.at[slot], ds_r.at[slot], before)

        @pl.when(core == 1)
        def _():
            send(deltas(slot, 0), deltas(slot, 1), dn_s.at[slot], dn_r.at[slot], other)

    def turn(j):
        dy = lax.div(j, 2)
        dy = dy + lax.div(dy, 2) - 2 * lax.div(dy, 3)
        return 2 * lax.rem(y + dy, NY) + lax.rem(j, 2)

    def pass_step(j, carry):
        pass_on(turn(j))
        return carry

    lax.fori_loop(0, SLOTS, pass_step, 0)
    at_place(6)

    over_z(0)

    took(qb.at[near, :], q_r.at[1])
    took(lse.at[2], row_r.at[0])

    @pl.when(core == 0)
    def _():
        send(lse.at[2], lse.at[1], row_s.at[1], row_r.at[1], other)

    took(lse.at[1], row_r.at[1])

    def later_head(i, carry):
        h = 8 * lax.rem(i, 2) + lax.div(i, 2)
        lanes = head_lanes(h)
        s = dot(kb[own, lanes], qb[TOK:, lanes], NT) * scale
        s = s + jnp.concatenate([bias[3], bias[4]], axis=1)
        probs_k[i] = jnp.exp(s - jnp.concatenate([lse[1, i], lse[2, i]], axis=1))
        return carry

    lax.fori_loop(0, HEADS, later_head, 0, unroll=UN)
    over_z(1)
    over_quarters(0)

    took(vb.at[prev2, :], kv_r.at[1])

    @pl.when(core == 1)
    def _():
        send(vb.at[prev2, :], vb.at[prev1, :], kv_s.at[3], kv_r.at[3], other)

    took(vb.at[prev1, :], kv_r.at[3])

    def own_head(i, carry):
        h = 8 * lax.rem(i, 2) + lax.div(i, 2)
        lanes = head_lanes(h)
        dprobs = dot(vb[:, lanes], dab[i, 0:TOK, :], NT)
        ds = (probs[i] * (dprobs - delta[0, i])).astype(BF)
        ds_own[i] = ds[0:TOK]
        dq_ref[:, lanes] = (dot(ds, kb[:, lanes], TN) * scale).astype(BF)
        return carry

    lax.fori_loop(0, HEADS, own_head, 0, unroll=UN)
    over_quarters(1)

    def key_head(i, carry):
        h = 8 * lax.rem(i, 2) + lax.div(i, 2)
        lanes = head_lanes(h)
        later = dab[i, TOK:, :]
        p = probs_k[i]
        dprobs = dot(vb[own, lanes], later, NT)
        ds = (p * (dprobs - jnp.concatenate([delta[1, i], delta[2, i]], axis=1))).astype(BF)
        dkey = dot(ds_own[i], qb[own, lanes], NN) + dot(ds, qb[TOK:, lanes], NN)
        dk_ref[:, lanes] = (dkey * scale).astype(BF)
        dval = dot(probs[i, 0:TOK, :].astype(BF), dab[i, 0:TOK, :], NN) + dot(p.astype(BF), later, NN)
        dv_ref[:, lanes] = dval.astype(BF)
        return carry


    def d_wo_sum():
        quarter_in[zq, zt] = jnp.zeros((32, 256), BF)
        took(zin.at[pl.ds(0, 3), 0, 0], rq_r)
        total = near_sum[zq, zt]
        for i in range(4):
            total = total + quarter_in[i // 2, i % 2].astype(F32)
        grad_scale = 1.0 / math.sqrt(8 * n_ctx * TOK)
        mine_f[...] = total * grad_scale
        for d in x_group:
            send(mine_f, fin.at[core * NX + x], rf_s, rf_r, x_peer(*d)[0])
        fin[core * NX + x] = mine_f[...]

    def from_next(slot):
        took(chunk(slot, far), fw_r.at[slot])
        took(deltas(slot, 2), ds_r.at[slot])

        @pl.when(core == 0)
        def _():
            send(chunk(slot, far), chunk(slot, near), fo_s.at[slot], fo_r.at[slot], other)
            send(deltas(slot, 2), deltas(slot, 1), dn_s.at[slot], dn_r.at[slot], other)

    def from_other(slot):
        took(chunk(slot, near), fo_r.at[slot])
        took(deltas(slot, 1), dn_r.at[slot])
        lax.fori_loop(2 * slot, 2 * slot + 2, key_head, 0)

    def key_step(j, carry):
        from_next(turn(j))
        from_other(turn(j - 1))
        return carry

    from_next(turn(0))
    lax.fori_loop(1, 6, key_step, 0)
    d_wo_sum()
    lax.fori_loop(6, SLOTS, key_step, 0)
    from_other(turn(SLOTS - 1))

    took(fin.at[pl.ds(0, 7)], rf_r)
    turned[...] = fin[...].reshape(2 * DH, 256).T
    dw_ref[...] = turned[pl.ds(pl.multiple_of((2 * x + core) * 32, 32), 32), :]

    took(wt_in.at[:, pl.ds(0, DH)], wc_s)
    for dz in Z_OFFSETS:
        took(w_piece(x, z), wz_s.at[dz])
    took(wt.at[:, :, pl.ds(0, 3)], wx_s)
    for part in range(2):
        for dx in (1, 3, 2):
            took(xin.at[part, dx], rx_s.at[part, dx])
    for part in range(2):
        for i in range(2):
            took(zin.at[i, part], rz_s.at[part, i])
            took(zin.at[2, part, i], rz_s.at[part, 2 + i])
        for top in range(2):
            @pl.when((zq != part) | (zt != top))
            def _():
                took(quarter_out.at[part, top], rq_s.at[part, top])
    took(fin.at[pl.ds(0, 7)], rf_s)
    for i in range(6):
        took(half(me, 0), g_s.at[i])
    for i in range(6, 10):
        took(whole(me), g_s.at[i])
    took(sb.at[pl.ds(0, 896), :], sa_s)
    for i in range(4):
        took(kb.at[own, :], kv_s.at[i])
    for i in range(2):
        took(lse.at[0], row_s.at[i])
    for i in range(2):
        took(qb.at[own, :], q_s.at[i])
    for slot in range(SLOTS):
        @pl.when(slot != me)
        def _():
            took(dsend.at[0], da_s.at[slot])

    for slot in range(SLOTS):
        took(chunk(slot, own), fw_s.at[slot])
        took(chunk(slot, own), fo_s.at[slot])
        took(deltas(slot, 0), ds_s.at[slot])
        took(deltas(slot, 0), dn_s.at[slot])


def per_device(queries, keys, values, saved_output, d_out, w_out, block_order):
    sems = pltpu.SemaphoreType.DMA
    vmem = pltpu.VMEM
    tokens = jax.ShapeDtypeStruct((TOK, FEAT), BF)
    anywhere = pl.BlockSpec(memory_space=pltpu.HBM)
    inside = pl.BlockSpec(memory_space=pltpu.VMEM)
    dq, dk, dv, dw = pl.pallas_call(
        kernel,
        out_shape=(tokens, tokens, tokens, jax.ShapeDtypeStruct((32, 256), F32)),
        in_specs=[pl.BlockSpec(memory_space=pltpu.SMEM)] + [anywhere] * 5 + [inside],
        out_specs=(inside,) * 4,
        scratch_shapes=[
            vmem((3 * TOK, FEAT), BF),
            vmem((3 * TOK, FEAT), BF),
            vmem((3 * TOK, FEAT), BF),
            vmem((TOK, FEAT), BF),
            vmem((SLOTS * TOK, FEAT), BF),
            vmem((HEADS, 3 * TOK, DH), BF),
            vmem((3, HEADS, 1, TOK), F32),
            vmem((3, HEADS, 1, TOK), F32),
            vmem((2, NZL, NX, 64, DH), BF),
            vmem((FEAT, 2 * DH), BF),
            vmem((SLOTS * TOK, 2 * DH), BF),
            vmem((2 * DH, SLOTS * TOK), BF),
            vmem((SLOTS, 2, TOK, DH), BF),
            vmem((HEADS, 3 * TOK, TOK), F32),
            vmem((HEADS, TOK, 2 * TOK), F32),
            vmem((HEADS, TOK, TOK), BF),
            vmem((5, TOK, TOK), F32),
            vmem((2, NX, 32, FEAT), F32),
            vmem((2, NX, 32, FEAT), BF),
            vmem((2, NX, 2, 32, 1024), BF),
            vmem((4, 2, 2, 32, 256), F32),
            vmem((4, 2, 2, 32, 256), BF),
            vmem((3, 2, 2, 32, 256), BF),
            vmem((2, 2, 32, 256), F32),
            vmem((2, 2, 32, 256), BF),
            vmem((2, 2, 32, 256), BF),
            vmem((32, 256), F32),
            vmem((2 * NX, 32, 256), F32),
            vmem((256, 2 * DH), F32),
            sems((5,)),
            sems,
            sems,
            sems((NZ,)),
            sems((NZ,)),
            sems,
            sems,
            sems((10,)),
            sems((10,)),
            sems,
            sems,
            sems((4,)),
            sems((4,)),
            sems((2,)),
            sems((2,)),
            sems((8,)),
            sems((8,)),
            sems((8,)),
            sems((8,)),
            sems((8,)),
            sems((8,)),
            sems((2,)),
            sems((2,)),
            sems((8,)),
            sems((8,)),
            sems((8,)),
            sems((8,)),
            sems((2, NX)),
            sems((2, NX)),
            sems((2, 4)),
            sems((2, 4)),
            sems((2, 2)),
            sems,
            sems,
            sems,
        ],
        compiler_params=pltpu.CompilerParams(
            collective_id=0, has_side_effects=True, vmem_limit_bytes=60 * 1024 * 1024
        ),
    )(block_order, queries[0], keys[0], values[0], saved_output[0], d_out[0], w_out.T)
    return dq[None], dk[None], dv[None], dw.T


def solution(mesh):
    tokens = P("dp", "ctx", None)
    return jax.shard_map(
        per_device,
        mesh=mesh,
        in_specs=(tokens,) * 5 + (P("dp", "ctx"), P()),
        out_specs=(tokens,) * 3 + (P("dp", "ctx"),),
        check_vma=False,
    )
```

time: 135 us -> 99.9 us (0.74)
  Pallas kernels: 124 us -> 94.1 us
  local copies, waits for them, and re-layouts: 9.64 us -> 4.58 us
    pallas_call x1, Pallas kernels: 124 us -> 94.1 us  [per_device(): pl.pallas_call(kernel, out_shape=(tokens, tokens, tokens, jax.ShapeDtypeS...]
    unnamed x18 -> x10, local copies, waits for them, and re-layouts: 9.64 us -> 4.58 us
where the time goes in v2:
time: 99.9 us; the launch traced here: 99.3 us
  Pallas kernels  94.1 us (94%)
  local copies, waits for them, and re-layouts  4.58 us (5%)
    pallas_call x1, Pallas kernels, per_device(): pl.pallas_call(kernel, out_shape=(tokens, tokens, tokens, jax.ShapeDtypeS...  94.1 us
    unnamed x10, local copies, waits for them, and re-layouts  4.58 us

profile of v2, /device:TPU:1, one launch (start us, length us, event | category | flops | bytes accessed | tf_op | source)
XLA Modules:
  0.0 99.3 jit_solution(16943246054075583634)
XLA Ops:
  0.6 94.1 %shard_map.102 = (bf16[128,2048]{1,0:T(8,128)(2,1)}, bf16[128,2048]{1,0:T(8,128)(2,1)}, bf16[128,2048]{1,0:T(8,128)(2,1)}, f32[32,256]{1,0:T(8,128)}) custom-call(s32[128]{0:T(128)} %order_ref.1, bf16[128,2048]{1,0:T(8,128)(2,1)} %bitcast.13, bf16[128,2048]{1,0:T(8,128)(2,1)} %bitcast.14, bf16[128,2048]{1,0:T(8,128)(2,1)} %bitcast.15, ...), custom_call_target="tpu_custom_call" | custom-call | tf_op jit(solution)/shard_map/pallas_call | solution.py:533
  94.7 0.0 copy-start.1
  94.7 1.9 %copy.15 = bf16[1,128,2048]{2,1,0:T(8,128)(2,1)} copy(bf16[1,128,2048]{2,1,0:T(8,128)(2,1)} %bitcast.12) | data formatting | bytes 1048576
  96.7 0.0 copy-done.1
  96.7 0.0 copy-start
  96.7 0.8 copy.16
  97.5 0.4 copy-done
  97.9 0.0 copy-start.2
  97.9 0.8 copy.17
  98.7 0.0 copy-done.2
  98.7 0.6 copy.18
Async XLA Ops:
  94.7 2.0 %copy-start.1 = (bf16[128,2048]{1,0:T(8,128)(2,1)S(1)}, bf16[128,2048]{1,0:T(8,128)(2,1)}, u32[]{:S(2)}) copy-start(bf16[128,2048]{1,0:T(8,128)(2,1)} %get-tuple-element.9) | copy-start | bytes 1572868
  96.7 1.2 %copy-start = (bf16[128,2048]{1,0:T(8,128)(2,1)S(1)}, bf16[128,2048]{1,0:T(8,128)(2,1)}, u32[]{:S(2)}) copy-start(bf16[128,2048]{1,0:T(8,128)(2,1)} %get-tuple-element.10) | copy-start | bytes 1572868
  97.9 0.8 copy-start.2

commit v3 on v2

--- a/solution.py
+++ b/solution.py
@@ -15,7 +15,7 @@
 SLOTS = 2 * NY
 Z_OFFSETS = (1, 15, 2, 14, 3, 13, 4, 12, 5, 11, 6, 10, 7, 9, 8)
 MESH = pl.DeviceIdType.MESH
-KQ, VV, KO, SA, UN = 1, 3, 2, 11, 4
+UNROLL = 4
 BF = jnp.bfloat16
 F32 = jnp.float32
 
@@ -137,28 +137,28 @@
     for zh in range(2):
         sb[my_rows, pl.ds(zh * DH, DH)] = sv[:, head_lanes(8 * zh + me)]
 
-    def at_place(n):
-        if n == KQ:
-            send(kb.at[own, :], kb.at[prev2, :], kv_s.at[0], kv_r.at[0], after)
-            send(qb.at[own, :], qb.at[prev2, :], q_s.at[0], q_r.at[0], before)
-        if n == VV:
-            send(vb.at[own, :], vb.at[prev2, :], kv_s.at[1], kv_r.at[1], after)
-        if n == KO:
-            @pl.when(core == 0)
-            def _():
-                send(kb.at[own, :], kb.at[prev1, :], kv_s.at[2], kv_r.at[2], other)
-                send(vb.at[own, :], vb.at[prev1, :], kv_s.at[3], kv_r.at[3], other)
-
-            @pl.when(core == 1)
-            def _():
-                send(qb.at[own, :], qb.at[prev1, :], q_s.at[1], q_r.at[1], other)
-        if n == SA:
-            for d in y_group:
-                dev, slot = y_peer(*d)
-                for top in range(2):
-                    send(sv.at[:, head_lanes(8 * top + slot)], sb.at[my_rows, pl.ds(top * DH, DH)], sa_s, sa_r, dev)
-
-    at_place(0)
+    def keys_and_queries(first, rows):
+        def part(start):
+            return pl.ds(start + first, rows)
+
+        @pl.when(x != NX - 1)
+        def _():
+            send(kb.at[part(0), :], kb.at[part(2 * TOK), :], kv_s.at[0], kv_r.at[0], after)
+
+        @pl.when(x != 0)
+        def _():
+            send(qb.at[part(0), :], qb.at[part(2 * TOK), :], q_s.at[0], q_r.at[0], before)
+
+    keys_and_queries(0, 32)
+
+    @pl.when(x == NX - 1)
+    def _():
+        send(kb.at[own, :], kb.at[prev2, :], kv_s.at[0], kv_r.at[0], after)
+
+    @pl.when(x == 0)
+    def _():
+        send(qb.at[own, :], qb.at[prev2, :], q_s.at[0], q_r.at[0], before)
+
 
     group = ctx
     lane = lax.broadcasted_iota(jnp.int32, (TOK, TOK), 1)
@@ -187,7 +187,7 @@
         probs[i, 0:TOK] = dot(kb[own, lanes], qb[own, lanes], NT) * scale + bias[0]
         return carry
 
-    lax.fori_loop(0, HEADS, own_scores, 0, unroll=UN)
+    lax.fori_loop(0, HEADS, own_scores, 0, unroll=UNROLL)
 
     def z_peer(dz):
         return at(x, y, lax.rem(z + dz, NZ), core)
@@ -204,23 +204,32 @@
         zz = lax.rem(z + dz, NZ)
         took(w_piece(x, zz), wz_r.at[NZ - dz])
         w_across(zz)
-        if KQ == 1 and i % 2 == 0:
-            part = i // 2 * 16
-            send(kb.at[pl.ds(part, 16), :], kb.at[pl.ds(2 * TOK + part, 16), :], kv_s.at[0], kv_r.at[0], after)
-            send(qb.at[pl.ds(part, 16), :], qb.at[pl.ds(2 * TOK + part, 16), :], q_s.at[0], q_r.at[0], before)
         if i == 5:
             took(half(s_down, 0), g_r.at[0])
             send(half(s_down, 0), half(s_down, 0), g_s.at[4], g_r.at[4], y_up)
             took(half(s_up, 1), g_r.at[1])
             send(half(s_up, 1), half(s_up, 1), g_s.at[5], g_r.at[5], y_down)
-            at_place(11)
-    at_place(2)
+            for d in y_group:
+                dev, slot = y_peer(*d)
+                for top in range(2):
+                    send(sv.at[:, head_lanes(8 * top + slot)], sb.at[my_rows, pl.ds(top * DH, DH)], sa_s, sa_r, dev)
+    keys_and_queries(32, 96)
+
+    @pl.when(core == 0)
+    def _():
+        send(kb.at[own, :], kb.at[prev1, :], kv_s.at[2], kv_r.at[2], other)
+        send(vb.at[own, :], vb.at[prev1, :], kv_s.at[3], kv_r.at[3], other)
+
+    @pl.when(core == 1)
+    def _():
+        send(qb.at[own, :], qb.at[prev1, :], q_s.at[1], q_r.at[1], other)
+
     took(half(s_down, 1), g_r.at[2])
     send(whole(s_down), whole(s_down), g_s.at[7], g_r.at[7], other)
     took(half(s_up, 0), g_r.at[3])
     send(whole(s_up), whole(s_up), g_s.at[8], g_r.at[8], other)
     took(wt.at[:, :, pl.ds(0, 3)], wx_r)
-    at_place(3)
+    send(vb.at[own, :], vb.at[prev2, :], kv_s.at[1], kv_r.at[1], after)
 
     took(half(s_far, 0), g_r.at[4])
     took(half(s_far, 1), g_r.at[5])
@@ -252,7 +261,6 @@
     for top in range(2):
         dab[2 * me + top, 0:TOK, :] = dsend[me, top]
 
-    at_place(4)
     took(sb.at[pl.ds(0, 896), :], sa_r)
     st[...] = sb[...].astype(F32).T.astype(BF)
 
@@ -275,7 +283,6 @@
                 at(xx, y, z, core),
             )
 
-    at_place(5)
 
     def over_z(part):
         sums = dwp[:, x, :, part_lanes(part)]
@@ -334,7 +341,7 @@
         lse[0, i] = top + jnp.log(total)
         return carry
 
-    lax.fori_loop(0, HEADS, score_head, 0, unroll=UN)
+    lax.fori_loop(0, HEADS, score_head, 0, unroll=UNROLL)
 
     near, far = pl.ds(TOK, TOK), pl.ds(2 * TOK, TOK)
     send(lse.at[0], lse.at[2], row_s.at[0], row_r.at[0], before)
@@ -385,7 +392,6 @@
         return carry
 
     lax.fori_loop(0, SLOTS, pass_step, 0)
-    at_place(6)
 
     over_z(0)
 
@@ -406,7 +412,7 @@
         probs_k[i] = jnp.exp(s - jnp.concatenate([lse[1, i], lse[2, i]], axis=1))
         return carry
 
-    lax.fori_loop(0, HEADS, later_head, 0, unroll=UN)
+    lax.fori_loop(0, HEADS, later_head, 0, unroll=UNROLL)
     over_z(1)
     over_quarters(0)
 
@@ -427,7 +433,7 @@
         dq_ref[:, lanes] = (dot(ds, kb[:, lanes], TN) * scale).astype(BF)
         return carry
 
-    lax.fori_loop(0, HEADS, own_head, 0, unroll=UN)
+    lax.fori_loop(0, HEADS, own_head, 0, unroll=UNROLL)
     over_quarters(1)
 
     def key_head(i, carry):
@@ -468,7 +474,8 @@
     def from_other(slot):
         took(chunk(slot, near), fo_r.at[slot])
         took(deltas(slot, 1), dn_r.at[slot])
-        lax.fori_loop(2 * slot, 2 * slot + 2, key_head, 0)
+        key_head(2 * slot, 0)
+        key_head(2 * slot + 1, 0)
 
     def key_step(j, carry):
         from_next(turn(j))

time: 99.9 us -> 96 us (0.961)
  Pallas kernels: 94.1 us -> 90.2 us
    pallas_call x1, Pallas kernels: 94.1 us -> 90.2 us  [per_device(): pl.pallas_call(kernel, out_shape=(tokens, tokens, tokens, jax.ShapeDtypeS...]
where the time goes in v3:
time: 96 us; the launch traced here: 95.5 us
  Pallas kernels  90.2 us (94%)
  local copies, waits for them, and re-layouts  4.58 us (5%)
    pallas_call x1, Pallas kernels, per_device(): pl.pallas_call(kernel, out_shape=(tokens, tokens, tokens, jax.ShapeDtypeS...  90.2 us
    unnamed x10, local copies, waits for them, and re-layouts  4.58 us

profile of v3, /device:TPU:1, one launch (start us, length us, event | category | flops | bytes accessed | tf_op | source)
XLA Modules:
  0.0 95.5 jit_solution(15719771486878250068)
XLA Ops:
  0.6 90.2 %shard_map.102 = (bf16[128,2048]{1,0:T(8,128)(2,1)}, bf16[128,2048]{1,0:T(8,128)(2,1)}, bf16[128,2048]{1,0:T(8,128)(2,1)}, f32[32,256]{1,0:T(8,128)}) custom-call(s32[128]{0:T(128)} %order_ref.1, bf16[128,2048]{1,0:T(8,128)(2,1)} %bitcast.13, bf16[128,2048]{1,0:T(8,128)(2,1)} %bitcast.14, bf16[128,2048]{1,0:T(8,128)(2,1)} %bitcast.15, ...), custom_call_target="tpu_custom_call" | custom-call | tf_op jit(solution)/shard_map/pallas_call | solution.py:540
  90.9 0.0 copy-start.1
  90.9 1.9 %copy.15 = bf16[1,128,2048]{2,1,0:T(8,128)(2,1)} copy(bf16[1,128,2048]{2,1,0:T(8,128)(2,1)} %bitcast.12) | data formatting | bytes 1048576
  92.8 0.0 copy-done.1
  92.8 0.0 copy-start
  92.8 0.8 copy.16
  93.6 0.4 copy-done
  94.1 0.0 copy-start.2
  94.1 0.8 copy.17
  94.9 0.0 copy-done.2
  94.9 0.6 copy.18
Async XLA Ops:
  90.9 2.0 %copy-start.1 = (bf16[128,2048]{1,0:T(8,128)(2,1)S(1)}, bf16[128,2048]{1,0:T(8,128)(2,1)}, u32[]{:S(2)}) copy-start(bf16[128,2048]{1,0:T(8,128)(2,1)} %get-tuple-element.9) | copy-start | bytes 1572868
  92.8 1.2 %copy-start = (bf16[128,2048]{1,0:T(8,128)(2,1)S(1)}, bf16[128,2048]{1,0:T(8,128)(2,1)}, u32[]{:S(2)}) copy-start(bf16[128,2048]{1,0:T(8,128)(2,1)} %get-tuple-element.10) | copy-start | bytes 1572868
  94.1 0.8 copy-start.2

commit v4 on v3

--- a/solution.py
+++ b/solution.py
@@ -15,7 +15,7 @@
 SLOTS = 2 * NY
 Z_OFFSETS = (1, 15, 2, 14, 3, 13, 4, 12, 5, 11, 6, 10, 7, 9, 8)
 MESH = pl.DeviceIdType.MESH
-UNROLL = 4
+UNROLL = 8
 BF = jnp.bfloat16
 F32 = jnp.float32
 
@@ -128,14 +128,10 @@
     prev2, prev1 = pl.ds(2 * TOK, TOK), pl.ds(TOK, TOK)
     loads[2].wait()
     loads[3].wait()
-    loads[4].wait()
-    loads[1].wait()
 
     def head_lanes(h):
         return pl.ds(pl.multiple_of(h * DH, DH), DH)
 
-    for zh in range(2):
-        sb[my_rows, pl.ds(zh * DH, DH)] = sv[:, head_lanes(8 * zh + me)]
 
     def keys_and_queries(first, rows):
         def part(start):
@@ -159,6 +155,10 @@
     def _():
         send(qb.at[own, :], qb.at[prev2, :], q_s.at[0], q_r.at[0], before)
 
+    loads[4].wait()
+    loads[1].wait()
+    for zh in range(2):
+        sb[my_rows, pl.ds(zh * DH, DH)] = sv[:, head_lanes(8 * zh + me)]
 
     group = ctx
     lane = lax.broadcasted_iota(jnp.int32, (TOK, TOK), 1)
@@ -257,7 +257,7 @@
                 )
         return carry
 
-    lax.fori_loop(0, 4, attn_step, 0)
+    lax.fori_loop(0, 4, attn_step, 0, unroll=2)
     for top in range(2):
         dab[2 * me + top, 0:TOK, :] = dsend[me, top]
 

time: 96 us -> 96.4 us (level)
  no operation moved by 1% of the time
where the time goes in v4:
time: 96.4 us; the launch traced here: 96.2 us
  Pallas kernels  90.9 us (94%)
  local copies, waits for them, and re-layouts  4.58 us (5%)
    pallas_call x1, Pallas kernels, per_device(): pl.pallas_call(kernel, out_shape=(tokens, tokens, tokens, jax.ShapeDtypeS...  90.9 us
    unnamed x10, local copies, waits for them, and re-layouts  4.58 us

profile of v4, /device:TPU:1, one launch (start us, length us, event | category | flops | bytes accessed | tf_op | source)
XLA Modules:
  0.0 96.2 jit_solution(7523719852745262319)
XLA Ops:
  0.6 90.9 %shard_map.102 = (bf16[128,2048]{1,0:T(8,128)(2,1)}, bf16[128,2048]{1,0:T(8,128)(2,1)}, bf16[128,2048]{1,0:T(8,128)(2,1)}, f32[32,256]{1,0:T(8,128)}) custom-call(s32[128]{0:T(128)} %order_ref.1, bf16[128,2048]{1,0:T(8,128)(2,1)} %bitcast.13, bf16[128,2048]{1,0:T(8,128)(2,1)} %bitcast.14, bf16[128,2048]{1,0:T(8,128)(2,1)} %bitcast.15, ...), custom_call_target="tpu_custom_call" | custom-call | tf_op jit(solution)/shard_map/pallas_call | solution.py:540
  91.6 0.0 copy-start.1
  91.6 1.9 %copy.15 = bf16[1,128,2048]{2,1,0:T(8,128)(2,1)} copy(bf16[1,128,2048]{2,1,0:T(8,128)(2,1)} %bitcast.12) | data formatting | bytes 1048576
  93.5 0.0 copy-done.1
  93.5 0.0 copy-start
  93.5 0.8 copy.16
  94.3 0.4 copy-done
  94.7 0.0 copy-start.2
  94.7 0.8 copy.17
  95.5 0.0 copy-done.2
  95.5 0.6 copy.18
Async XLA Ops:
  91.6 2.0 %copy-start.1 = (bf16[128,2048]{1,0:T(8,128)(2,1)S(1)}, bf16[128,2048]{1,0:T(8,128)(2,1)}, u32[]{:S(2)}) copy-start(bf16[128,2048]{1,0:T(8,128)(2,1)} %get-tuple-element.9) | copy-start | bytes 1572868
  93.5 1.2 %copy-start = (bf16[128,2048]{1,0:T(8,128)(2,1)S(1)}, bf16[128,2048]{1,0:T(8,128)(2,1)}, u32[]{:S(2)}) copy-start(bf16[128,2048]{1,0:T(8,128)(2,1)} %get-tuple-element.10) | copy-start | bytes 1572868
  94.7 0.8 copy-start.2
